TPU v7x, 32 devices: a whole 2x2x4 slice. The times are simulated.
32 devices in a mesh: node: 4 (over x, core), wide: 8 (over z, y).
Axes of the slice: x: 2, y: 2, z: 4, core: 2. Of those that a mesh axis runs over, the one named last changes fastest.
Arguments:
- tokens: bfloat16 [2048, 4096], P(('node', 'wide')), may hold values from -6 to 6
- expert_ids: int32 [2048, 6], P(('node', 'wide')), may hold values from 0 to 31, all different within a row; in each aligned block of 64 rows (0 to 63, 64 to 127, ...) at most 16 rows name the same one
- gate_weights: float32 [2048, 6], P(('node', 'wide')), may hold values from 0.1 to 1
- w_gate: bfloat16 [32, 4096, 768], P(('node', 'wide')), may hold values from -0.09375 to 0.09375
- w_up: bfloat16 [32, 4096, 768], P(('node', 'wide')), may hold values from -0.09375 to 0.09375
- w_down: bfloat16 [32, 768, 4096], P(('node', 'wide')), may hold values from -0.21875 to 0.21875
- gate_scale: float32 [32, 768], P(('node', 'wide')), may hold values from 0.5 to 2
- up_scale: float32 [32, 768], P(('node', 'wide')), may hold values from 0.5 to 2
- down_scale: float32 [32, 4096], P(('node', 'wide')), may hold values from 0.5 to 2
Outputs:
- mixed: bfloat16 [2048, 4096], P(('node', 'wide'))
Inputs may be any that keep to these rules, and one draw needn't show every extreme that they name: `expert_ids`: each token names 6 different experts; among the routes of the tokens of one device no expert is named more than 16 times, a bound that some block reaches.
All inputs are finite; a program needn't handle non-finite values.
Results may differ from a plain program's by a relative error of at most 0.0058.
Values may be sent and summed in bfloat16 or wider, within the bound.
A program may use at most 128 MiB of HBM per device.

v0:
```python
import jax
import jax.numpy as jnp
from jax import lax
from jax.sharding import PartitionSpec as P


def expert_block(received, w_gate, w_up, w_down, gate_scale, up_scale, down_scale):
    shape = received.shape
    rows = received.reshape(-1, shape[-1])
    gate = jnp.dot(rows, w_gate[0], preferred_element_type=jnp.float32) * gate_scale[0]
    up = jnp.dot(rows, w_up[0], preferred_element_type=jnp.float32) * up_scale[0]
    hidden = (jax.nn.silu(gate) * up).astype(jnp.bfloat16)
    routed = jnp.dot(hidden, w_down[0], preferred_element_type=jnp.float32) * down_scale[0]
    return routed.astype(jnp.bfloat16).reshape(shape)


def on_device(
    tokens, expert_ids, gate_weights, w_gate, w_up, w_down, gate_scale, up_scale, down_scale
):
    count, top = expert_ids.shape
    width = tokens.shape[1]
    experts = lax.axis_size(("node", "wide"))
    capacity = max(2, 4 * count * top // (3 * experts))
    flat_ids = expert_ids.reshape(-1)
    picked = (flat_ids[:, None] == jnp.arange(experts, dtype=jnp.int32)[None, :]).astype(jnp.int32)
    before = jnp.cumsum(picked, axis=0) - picked
    position = jnp.sum(before * picked, axis=1)
    slots = flat_ids * capacity + position
    place = slots[:, None] == jnp.arange(experts * capacity, dtype=jnp.int32)[None, :]
    dispatch = jnp.sum(
        place.reshape(count, top, experts * capacity).astype(jnp.float32), axis=1
    ).astype(jnp.bfloat16)
    packed = lax.dot_general(
        dispatch, tokens, (((0,), (0,)), ((), ())), preferred_element_type=jnp.float32
    )
    packed = packed.astype(jnp.bfloat16).reshape(experts, capacity, width)
    returned = lax.all_to_all(
        expert_block(
            lax.all_to_all(packed, ("node", "wide"), split_axis=0, concat_axis=0, tiled=True),
            w_gate,
            w_up,
            w_down,
            gate_scale,
            up_scale,
            down_scale,
        ),
        ("node", "wide"),
        split_axis=0,
        concat_axis=0,
        tiled=True,
    )
    results = returned.reshape(experts * capacity, width)
    chosen = results[slots].reshape(count, top, width).astype(jnp.float32)
    mixed = jnp.sum(chosen * gate_weights[:, :, None], axis=1)
    return mixed.astype(jnp.bfloat16)


def solution(mesh):
    placed = (
        P(("node", "wide"), None),
        P(("node", "wide"), None),
        P(("node", "wide"), None),
        P(("node", "wide"), None, None),
        P(("node", "wide"), None, None),
        P(("node", "wide"), None, None),
        P(("node", "wide"), None),
        P(("node", "wide"), None),
        P(("node", "wide"), None),
    )
    return jax.shard_map(
        on_device, mesh=mesh, in_specs=placed, out_specs=P(("node", "wide"), None), check_vma=False
    )
```

profile of v0, /device:TPU:0, one launch (start us, length us, event | category | flops | bytes accessed | tf_op | source)
XLA Modules:
  0.0 257.2 jit_solution(17395395365199967782)
XLA Ops:
  0.0 0.0 copy-start
  0.0 0.8 copy.17
  0.8 0.1 eq.43
  1.0 0.1 eq.39
  1.1 0.9 reduce-window.6
  2.0 0.2 slice_reduce_fusion
  2.3 0.1 fusion.12
  2.4 0.1 reduce_sum.32
  2.5 0.1 copy.21
  2.6 0.2 convert_reduce_fusion
  2.8 0.0 copy-done
  2.8 3.2 %convolution_convert_fusion = bf16[512,4096]{1,0:T(8,128)(2,1)} fusion(bf16[64,4096]{1,0:T(8,128)(2,1)S(1)} %copy-done, bf16[64,512]{1,0:T(8,128)(2,1)S(1)} %convert_reduce_fusion), kind=kOutput, calls=%fused_computation.8 | convolution fusion | flops 270532608 | bytes 4784128 | tf_op jit(solution)/shard_map/dot_general | solution.py:33
  6.0 0.0 copy-start.2
  6.0 0.0 copy-start.3
  6.0 7.4 %all-to-all-start = ((bf16[32,16,4096]{2,1,0:T(8,128)(2,1)}), bf16[32,16,4096]{2,1,0:T(8,128)(2,1)}, u32[]{:S(2)}, u32[]{:S(2)}) async-start(bf16[32,16,4096]{2,1,0:T(8,128)(2,1)} %bitcast.42), calls=%async_computation | async-start | bytes 8388608 | tf_op jit(solution)/shard_map/all_to_all | solution.py:39
  13.5 0.0 copy-done.2
  13.5 0.0 copy-done.3
  13.5 95.9 %all-to-all-done = bf16[32,16,4096]{2,1,0:T(8,128)(2,1)} async-done(((bf16[32,16,4096]{2,1,0:T(8,128)(2,1)}), bf16[32,16,4096]{2,1,0:T(8,128)(2,1)}, u32[]{:S(2)}, u32[]{:S(2)}) %all-to-all-start) | async-done | bytes 4194336 | tf_op jit(solution)/shard_map/all_to_all | solution.py:39
  109.4 0.0 copy-start.4
  109.4 7.0 %fusion.1 = f32[512,768]{1,0:T(8,128)S(1)} fusion(bf16[512,4096]{1,0:T(8,128)(2,1)} %bitcast.2, bf16[1,4096,768]{2,1,0:T(8,128)(2,1)} %param.13), kind=kOutput, calls=%fused_computation.4 | convolution fusion | flops 3221225472 | bytes 12058624 | tf_op jit(solution)/shard_map/dot_general | solution.py:11
  116.5 0.0 copy-done.4
  116.5 16.7 %multiply_convert_fusion = bf16[512,4096]{1,0:T(8,128)(2,1)} fusion(bf16[1,768,4096]{2,1,0:T(8,128)(2,1)} %param.14, f32[4096]{0:T(1024)S(1)} %bitcast.45, f32[512,768]{1,0:T(8,128)S(1)} %fusion.1, bf16[512,4096]{1,0:T(8,128)(2,1)} %bitcast.2, bf16[1,4096,768]{2,1,0:T(8,128)(2,1)} %param.12, f32[768]{0:T(1024)S(1)} %reduce.2, f32[768]{0:T(1024)S(1)} %reduce.1), kind=kOutput, calls=%fused_computation.2 | convolution fusion | flops 6449790976 | bytes 22566912 | tf_op jit(solution)/shard_map/dot_general | solution.py:13
  133.2 0.0 copy-start.1
  133.2 3.9 %all-to-all-start.1 = ((bf16[32,16,4096]{2,1,0:T(8,128)(2,1)}), bf16[32,16,4096]{2,1,0:T(8,128)(2,1)}, u32[]{:S(2)}, u32[]{:S(2)}) async-start(bf16[32,16,4096]{2,1,0:T(8,128)(2,1)} %bitcast.43), calls=%async_computation.1 | async-start | bytes 8388608 | tf_op jit(solution)/shard_map/all_to_all | solution.py:37
  137.0 0.1 mul.81
  137.2 0.0 copy-done.1
  137.2 0.1 copy.22
  137.3 95.5 %all-to-all-done.1 = bf16[32,16,4096]{2,1,0:T(8,128)(2,1)} async-done(((bf16[32,16,4096]{2,1,0:T(8,128)(2,1)}), bf16[32,16,4096]{2,1,0:T(8,128)(2,1)}, u32[]{:S(2)}, u32[]{:S(2)}) %all-to-all-start.1) | async-done | bytes 4194336 | tf_op jit(solution)/shard_map/all_to_all | solution.py:37
  232.8 11.0 %gather_fusion = bf16[384,4096]{1,0:T(8,128)(2,1)} fusion(bf16[512,4096]{1,0:T(8,128)(2,1)} %bitcast.8, s32[1024]{0:T(1024)S(1)} %pad_clamp_fusion), kind=kCustom, calls=%fused_computation | custom fusion | bytes 6292992 | tf_op jit(solution)/shard_map/gather | solution.py:53
  243.8 6.0 %reshape.81 = f32[64,6,4096]{2,1,0:T(8,128)} reshape(bf16[384,4096]{1,0:T(8,128)(2,1)} %gather_fusion) | data formatting | bytes 9437184 | tf_op jit(solution)/shard_map/convert_element_type | solution.py:53
  249.8 7.3 %multiply_reduce_fusion = bf16[64,4096]{1,0:T(8,128)(2,1)} fusion(f32[64,6,4096]{2,1,0:T(8,128)} %reshape.81, f32[64,6]{1,0:T(8,128)S(1)} %copy.22), kind=kLoop, calls=%fused_computation.1 | loop fusion | flops 2883584 | bytes 6817280 | tf_op jit(solution)/shard_map/reduce_sum | solution.py:54
  (7 shorter events, 0.1 us)
Async XLA Ops:
  0.0 2.8 %copy-start = (bf16[64,4096]{1,0:T(8,128)(2,1)S(1)}, bf16[64,4096]{1,0:T(8,128)(2,1)}, u32[]{:S(2)}) copy-start(bf16[64,4096]{1,0:T(8,128)(2,1)} %param.9) | copy-start | bytes 1572868
  6.0 7.4 %copy-start.2 = (f32[1,768]{1,0:T(1,128)S(1)}, f32[1,768]{1,0:T(1,128)}, u32[]{:S(2)}) copy-start(f32[1,768]{1,0:T(1,128)} %param.15) | copy-start | bytes 9220
  6.0 7.5 %copy-start.3 = (f32[1,768]{1,0:T(1,128)S(1)}, f32[1,768]{1,0:T(1,128)}, u32[]{:S(2)}) copy-start(f32[1,768]{1,0:T(1,128)} %param.16) | copy-start | bytes 9220
  6.0 103.4 %all-to-all-start = ((bf16[32,16,4096]{2,1,0:T(8,128)(2,1)}), bf16[32,16,4096]{2,1,0:T(8,128)(2,1)}, u32[]{:S(2)}, u32[]{:S(2)}) async-start(bf16[32,16,4096]{2,1,0:T(8,128)(2,1)} %bitcast.42), calls=%async_computation | async-start | bytes 8388608 | tf_op jit(solution)/shard_map/all_to_all | solution.py:39
  109.4 7.1 %copy-start.4 = (f32[1,4096]{1,0:T(1,128)S(1)}, f32[1,4096]{1,0:T(1,128)}, u32[]{:S(2)}) copy-start(f32[1,4096]{1,0:T(1,128)} %param.17) | copy-start | bytes 49156
  133.2 4.0 %copy-start.1 = (f32[64,6]{0,1:T(8,128)S(1)}, f32[64,6]{0,1:T(8,128)}, u32[]{:S(2)}) copy-start(f32[64,6]{0,1:T(8,128)} %param.11) | copy-start | bytes 4612
  133.2 99.7 %all-to-all-start.1 = ((bf16[32,16,4096]{2,1,0:T(8,128)(2,1)}), bf16[32,16,4096]{2,1,0:T(8,128)(2,1)}, u32[]{:S(2)}, u32[]{:S(2)}) async-start(bf16[32,16,4096]{2,1,0:T(8,128)(2,1)} %bitcast.43), calls=%async_computation.1 | async-start | bytes 8388608 | tf_op jit(solution)/shard_map/all_to_all | solution.py:37
where the time goes:
time: 258 us; the launch traced here: 257 us
  waiting for transfers between devices  191 us (74%)
  matrix products  26.9 us (10%)
  local copies, waits for them, and re-layouts  18.8 us (7%)
  starting transfers between devices  11.3 us (4%)
  other arithmetic  8.58 us (3%)
    all_to_all x1, waiting for transfers between devices, on_device(): lax.all_to_all(packed, ('node', 'wide'), split_axis=0, concat_axis=0, til...  95.9 us
    all_to_all x1, waiting for transfers between devices, on_device(): lax.all_to_all(expert_block(lax.all_to_all(packed, ('node', 'wide'), spli...  95.5 us
    dot_general x1, matrix products, expert_block(): jnp.dot(hidden, w_down[0], preferred_element_type=jnp.float32)  16.7 us
    gather x1, local copies, waits for them, and re-layouts, on_device(): chosen = results[slots].reshape(count, top, width).astype(jnp.float32)  11 us
    all_to_all x1, starting transfers between devices, on_device(): lax.all_to_all(packed, ('node', 'wide'), split_axis=0, concat_axis=0, til...  7.43 us
    reduce_sum x1, other arithmetic, on_device(): mixed = jnp.sum(chosen * gate_weights[:, :, None], axis=1)  7.33 us
    dot_general x1, matrix products, expert_block(): jnp.dot(rows, w_up[0], preferred_element_type=jnp.float32) * up_scale[0]  7.04 us
    convert_element_type x1, local copies, waits for them, and re-layouts, on_device(): chosen = results[slots].reshape(count, top, width).astype(jnp.float32)  6.03 us
  transfers between devices with their start and end apart: 2, of which 2 were waited for; matrix products, arithmetic and copies ran while one was open for 0% of the time, Pallas kernels for 0%

commit v1 on v0

v1 whole, which is shorter than its diff:
```python
import functools
import math

import jax
import jax.numpy as jnp
from jax import lax
from jax.experimental import pallas as pl
from jax.experimental.pallas import tpu as pltpu
from jax.sharding import PartitionSpec as P

MESH = pl.DeviceIdType.MESH
CHUNKS = 8
LAG = 1


def tile_of(size, most):
    return most if size % most == 0 else size


def kernel(
    groups,
    ring,
    tok_ref,
    meta_ref,
    gate_hbm,
    up_hbm,
    down_hbm,
    gate_scale_ref,
    up_scale_ref,
    down_scale_ref,
    out_ref,
    metas,
    tokens,
    packed,
    rows,
    w_gate,
    w_up,
    w_down,
    gate,
    up,
    hidden,
    results,
    returned,
    partial,
    partials,
    dispatch,
    weighted,
    combine,
    meta_sems,
    weight_sems,
    out_z,
    in_z,
    own_z,
    out_p,
    in_p,
    own_p,
    back_out_p,
    back_in_p,
    back_own_p,
    back_out_z,
    back_in_z,
    back_own_z,
):
    chunks, _, cols = tokens.shape
    count = tok_ref.shape[0]
    members = metas.shape[1] // 2
    slots = packed.shape[1] // members
    node, wide = lax.axis_index("node"), lax.axis_index("wide")
    my_group, my_ring = lax.div(wide, ring), lax.rem(wide, ring)
    me = node * ring + my_ring

    def group_at(i):
        return lax.rem(my_group + i, groups)

    def group_id(g):
        return (node, g * ring + my_ring)

    def member_at(i):
        return lax.rem(me + i, members)

    def member_id(d):
        return (lax.div(d, ring), my_group * ring + lax.rem(d, ring))

    def part(index, size):
        return pl.ds(pl.multiple_of(index * size, size), size)

    def arrived(ref, sem):
        pltpu.make_async_copy(ref, ref, sem).wait()

    weights = [
        pltpu.make_async_copy(gate_hbm.at[0], w_gate, weight_sems.at[0]),
        pltpu.make_async_copy(up_hbm.at[0], w_up, weight_sems.at[1]),
        pltpu.make_async_copy(down_hbm.at[0], w_down, weight_sems.at[2]),
    ]

    barrier = pltpu.get_barrier_semaphore()

    @pl.loop(1, groups)
    def _(i):
        pl.semaphore_signal(barrier, inc=1, device_id=group_id(group_at(i)), device_id_type=MESH)

    @pl.loop(1, members)
    def _(i):
        pl.semaphore_signal(barrier, inc=1, device_id=member_id(member_at(i)), device_id_type=MESH)

    for w in weights:
        w.start()
    pl.semaphore_wait(barrier, groups + members - 2)

    @pl.loop(1, groups)
    def _(i):
        g = group_at(i)
        pltpu.make_async_remote_copy(
            src_ref=meta_ref.at[g],
            dst_ref=metas.at[my_group],
            send_sem=meta_sems.at[0],
            recv_sem=meta_sems.at[1],
            device_id=group_id(g),
            device_id_type=MESH,
        ).start()

    @pl.loop(0, chunks)
    def _(c):
        mine = tok_ref.at[:, part(c, cols)]
        place = tokens.at[c, part(my_group, count)]

        @pl.loop(1, groups)
        def _(i):
            pltpu.make_async_remote_copy(
                src_ref=mine,
                dst_ref=place,
                send_sem=out_z.at[c],
                recv_sem=in_z.at[c],
                device_id=group_id(group_at(i)),
                device_id_type=MESH,
            ).start()

        pltpu.make_async_copy(mine, place, own_z.at[c]).start()

    gate[...] = jnp.zeros_like(gate)
    up[...] = jnp.zeros_like(up)

    own_meta = pltpu.make_async_copy(meta_ref.at[my_group], metas.at[my_group], meta_sems.at[2])
    own_meta.start()
    own_meta.wait()
    arrived(metas.at[pl.ds(0, groups - 1)], meta_sems.at[1])
    place = jnp.max(metas[:, :members, :], axis=0)
    weight = jnp.sum(metas[:, members:, :], axis=0)
    slot = lax.broadcasted_iota(jnp.int32, (slots, groups * count), 0).astype(jnp.float32)
    for d in range(members):
        same = place[d : d + 1, :] == slot
        dispatch[pl.ds(d * slots, slots), :] = jnp.where(same, 1.0, 0.0).astype(jnp.bfloat16)
        weighted[pl.ds(d * slots, slots), :] = jnp.where(same, weight[d : d + 1, :], 0.0)
    combine[...] = weighted[...].T.astype(jnp.bfloat16)

    half = tile_of(cols, 256)

    def pack(c):
        pltpu.make_async_copy(
            tok_ref.at[:, part(c, cols)], tokens.at[c, part(my_group, count)], own_z.at[c]
        ).wait()
        arrived(tokens.at[c, pl.ds(0, (groups - 1) * count)], in_z.at[c])

        @pl.loop(0, cols // half)
        def _(j):
            packed[c, :, part(j, half)] = jnp.dot(
                dispatch[...], tokens[c, :, part(j, half)], preferred_element_type=jnp.float32
            ).astype(jnp.bfloat16)

        @pl.loop(1, members)
        def _(i):
            d = member_at(i)
            pltpu.make_async_remote_copy(
                src_ref=packed.at[c, part(d, slots)],
                dst_ref=rows.at[c, part(me, slots)],
                send_sem=out_p.at[c],
                recv_sem=in_p.at[c],
                device_id=member_id(d),
                device_id_type=MESH,
            ).start()

        pltpu.make_async_copy(
            packed.at[c, part(me, slots)], rows.at[c, part(me, slots)], own_p.at[c]
        ).start()

    wide_tile = tile_of(gate.shape[1], 256)

    def project(c):
        pltpu.make_async_copy(
            packed.at[c, part(me, slots)], rows.at[c, part(me, slots)], own_p.at[c]
        ).wait()
        arrived(rows.at[c, pl.ds(0, (members - 1) * slots)], in_p.at[c])

        @pl.loop(0, gate.shape[1] // wide_tile)
        def _(j):
            at = part(j, wide_tile)
            gate[:, at] += jnp.dot(
                rows[c], w_gate[part(c, cols), at], preferred_element_type=jnp.float32
            )
            up[:, at] += jnp.dot(
                rows[c], w_up[part(c, cols), at], preferred_element_type=jnp.float32
            )

    @pl.loop(0, LAG)
    def _(c):
        pack(c)

    weights[0].wait()
    weights[1].wait()

    @pl.loop(LAG, chunks)
    def _(c):
        pack(c)
        project(c - LAG)

    weights[2].wait()

    @pl.loop(chunks - LAG, chunks)
    def _(c):
        project(c)

    @pl.loop(0, gate.shape[1] // wide_tile)
    def _(j):
        at = part(j, wide_tile)
        g = gate[:, at] * gate_scale_ref[:, at]
        hidden[:, at] = (g / (1.0 + jnp.exp(-g)) * (up[:, at] * up_scale_ref[:, at])).astype(jnp.bfloat16)

    @pl.loop(0, chunks)
    def _(c):
        @pl.loop(0, cols // half)
        def _(j):
            at = part(c * (cols // half) + j, half)
            results[c, :, part(j, half)] = (
                jnp.dot(hidden[...], w_down[:, at], preferred_element_type=jnp.float32)
                * down_scale_ref[:, at]
            ).astype(jnp.bfloat16)

        @pl.loop(1, members)
        def _(i):
            d = member_at(i)
            pltpu.make_async_remote_copy(
                src_ref=results.at[c, part(d, slots)],
                dst_ref=returned.at[c, part(me, slots)],
                send_sem=back_out_p.at[c],
                recv_sem=back_in_p.at[c],
                device_id=member_id(d),
                device_id_type=MESH,
            ).start()

        pltpu.make_async_copy(
            results.at[c, part(me, slots)], returned.at[c, part(me, slots)], back_own_p.at[c]
        ).start()

    @pl.loop(0, chunks)
    def _(c):
        pltpu.make_async_copy(
            results.at[c, part(me, slots)], returned.at[c, part(me, slots)], back_own_p.at[c]
        ).wait()
        arrived(returned.at[c, pl.ds(0, (members - 1) * slots)], back_in_p.at[c])

        @pl.loop(0, cols // half)
        def _(j):
            partial[c, :, part(j, half)] = jnp.dot(
                combine[...], returned[c, :, part(j, half)], preferred_element_type=jnp.float32
            ).astype(jnp.bfloat16)

        @pl.loop(1, groups)
        def _(i):
            g = group_at(i)
            pltpu.make_async_remote_copy(
                src_ref=partial.at[c, part(g, count)],
                dst_ref=partials.at[c, part(my_group, count)],
                send_sem=back_out_z.at[c],
                recv_sem=back_in_z.at[c],
                device_id=group_id(g),
                device_id_type=MESH,
            ).start()

        pltpu.make_async_copy(
            partial.at[c, part(my_group, count)],
            partials.at[c, part(my_group, count)],
            back_own_z.at[c],
        ).start()

    @pl.loop(0, chunks)
    def _(c):
        pltpu.make_async_copy(
            partial.at[c, part(my_group, count)],
            partials.at[c, part(my_group, count)],
            back_own_z.at[c],
        ).wait()
        arrived(partials.at[c, pl.ds(0, (groups - 1) * count)], back_in_z.at[c])
        total = partials[c, pl.ds(0, count), :].astype(jnp.float32)
        for g in range(1, groups):
            total += partials[c, pl.ds(g * count, count), :].astype(jnp.float32)
        out_ref[:, part(c, cols)] = total.astype(jnp.bfloat16)

    arrived(metas.at[pl.ds(0, groups - 1)], meta_sems.at[0])

    @pl.loop(0, chunks)
    def _(c):
        arrived(tokens.at[c, pl.ds(0, (groups - 1) * count)], out_z.at[c])
        arrived(packed.at[c, pl.ds(0, (members - 1) * slots)], out_p.at[c])
        arrived(results.at[c, pl.ds(0, (members - 1) * slots)], back_out_p.at[c])
        arrived(partial.at[c, pl.ds(0, (groups - 1) * count)], back_out_z.at[c])


def on_device(
    tokens, expert_ids, gate_weights, w_gate, w_up, w_down, gate_scale, up_scale, down_scale
):
    count, top = expert_ids.shape
    width = tokens.shape[1]
    inner = w_gate.shape[2]
    nodes, wides = lax.axis_size("node"), lax.axis_size("wide")
    experts = nodes * wides
    capacity = max(2, 4 * count * top // (3 * experts))
    groups = math.gcd(4, wides)
    ring = wides // groups
    members = nodes * ring
    slots = groups * capacity
    held = groups * count
    chunks = CHUNKS
    cols = width // chunks

    my_group = lax.axis_index("wide") // ring
    named = expert_ids.T[:, None, :] == jnp.arange(experts, dtype=jnp.int32)[None, :, None]
    picked = jnp.any(named, axis=0)
    weight = jnp.sum(jnp.where(named, gate_weights.T[:, None, :], 0.0), axis=0)
    earlier = jnp.arange(count)[:, None] < jnp.arange(count)[None, :]
    position = jnp.dot(
        picked.astype(jnp.bfloat16), earlier.astype(jnp.bfloat16), preferred_element_type=jnp.float32
    )
    place = jnp.where(picked, position + (my_group * capacity).astype(jnp.float32), -1.0)
    here = (jnp.arange(held) // count == my_group)[None, :]
    place = jnp.where(here, jnp.tile(place, (1, groups)), -1.0)
    weight = jnp.where(here, jnp.tile(weight, (1, groups)), 0.0)
    meta = jnp.stack([place, weight]).reshape(2, nodes, groups, ring, held)
    meta = meta.transpose(2, 0, 1, 3, 4).reshape(groups, 2 * members, held)

    vmem = pl.BlockSpec(memory_space=pltpu.VMEM)
    anywhere = pl.BlockSpec(memory_space=pl.ANY)
    rows = members * slots
    bf16, f32 = jnp.bfloat16, jnp.float32
    per_chunk = pltpu.SemaphoreType.DMA((chunks,))
    return pl.pallas_call(
        functools.partial(kernel, groups, ring),
        out_shape=jax.ShapeDtypeStruct((count, width), bf16),
        in_specs=[vmem, vmem, anywhere, anywhere, anywhere, vmem, vmem, vmem],
        out_specs=vmem,
        scratch_shapes=[
            pltpu.VMEM((groups, 2 * members, held), f32),
            pltpu.VMEM((chunks, held, cols), bf16),
            pltpu.VMEM((chunks, rows, cols), bf16),
            pltpu.VMEM((chunks, rows, cols), bf16),
            pltpu.VMEM((width, inner), bf16),
            pltpu.VMEM((width, inner), bf16),
            pltpu.VMEM((inner, width), bf16),
            pltpu.VMEM((rows, inner), f32),
            pltpu.VMEM((rows, inner), f32),
            pltpu.VMEM((rows, inner), bf16),
            pltpu.VMEM((chunks, rows, cols), bf16),
            pltpu.VMEM((chunks, rows, cols), bf16),
            pltpu.VMEM((chunks, held, cols), bf16),
            pltpu.VMEM((chunks, held, cols), bf16),
            pltpu.VMEM((rows, held), bf16),
            pltpu.VMEM((rows, held), f32),
            pltpu.VMEM((held, rows), bf16),
            pltpu.SemaphoreType.DMA((3,)),
            pltpu.SemaphoreType.DMA((3,)),
        ]
        + [per_chunk] * 12,
        compiler_params=pltpu.CompilerParams(
            collective_id=0, has_side_effects=True, vmem_limit_bytes=60 * 2**20
        ),
    )(tokens, meta, w_gate, w_up, w_down, gate_scale, up_scale, down_scale)


def solution(mesh):
    placed = (
        P(("node", "wide"), None),
        P(("node", "wide"), None),
        P(("node", "wide"), None),
        P(("node", "wide"), None, None),
        P(("node", "wide"), None, None),
        P(("node", "wide"), None, None),
        P(("node", "wide"), None),
        P(("node", "wide"), None),
        P(("node", "wide"), None),
    )
    return jax.shard_map(
        on_device, mesh=mesh, in_specs=placed, out_specs=P(("node", "wide"), None), check_vma=False
    )
```

time: 258 us -> 134 us (0.52)
  waiting for transfers between devices: 191 us -> 0 us
  Pallas kernels: 0 us -> 129 us
  matrix products: 26.9 us -> 0.13 us
  local copies, waits for them, and re-layouts: 18.8 us -> 2.79 us
  starting transfers between devices: 11.3 us -> 0 us
  other arithmetic: 8.58 us -> 1.51 us
    all_to_all x2 -> x0, waiting for transfers between devices: 191 us -> none  [the longest x1 95.9 us: on_device(): lax.all_to_all(packed, ('node', 'wide'), split_axis=0, concat_axis=0, til...]
    pallas_call x0 -> x1, Pallas kernels: none -> 129 us  [on_device(): pl.pallas_call(functools.partial(kernel, groups, ring), out_shape=jax.Sha...]
    dot_general x3 -> x1, matrix products: 26.9 us -> 0.13 us  [on_device(): jnp.dot(picked.astype(jnp.bfloat16), earlier.astype(jnp.bfloat16), prefer...]
    all_to_all x2 -> x0, starting transfers between devices: 11.3 us -> none  [the longest x1 7.43 us: on_device(): lax.all_to_all(packed, ('node', 'wide'), split_axis=0, concat_axis=0, til...]
    gather x1 -> x0, local copies, waits for them, and re-layouts: 11 us -> none  [on_device(): chosen = results[slots].reshape(count, top, width).astype(jnp.float32)]
    reduce_sum x3 -> x1, other arithmetic: 7.59 us -> 0.73 us  [on_device(): weight = jnp.sum(jnp.where(named, gate_weights.T[:, None, :], 0.0), axis=0)]
    convert_element_type x1 -> x0, local copies, waits for them, and re-layouts: 6.03 us -> none  [on_device(): chosen = results[slots].reshape(count, top, width).astype(jnp.float32)]
  transfers between devices with their start and end apart: 2 -> 0, of which waited for: 2 -> 0; matrix products, arithmetic and copies ran while one was open for 0% -> 0% of each run, Pallas kernels for 0% -> 0%
where the time goes in v1:
time: 134 us; the launch traced here: 133 us
  Pallas kernels  129 us (96%)
  local copies, waits for them, and re-layouts  2.79 us (2%)
  other arithmetic  1.51 us (1%)
    pallas_call x1, Pallas kernels, on_device(): pl.pallas_call(functools.partial(kernel, groups, ring), out_shape=jax.Sha...  129 us

profile of v1, /device:TPU:0, one launch (start us, length us, event | category | flops | bytes accessed | tf_op | source)
XLA Modules:
  0.0 133.5 jit_solution(8212245643279183556)
XLA Ops:
  0.0 0.7 fusion.1
  0.7 0.1 fusion
  0.8 0.7 select_reduce_fusion
  1.6 0.1 tile.21
  1.7 0.1 tile.9
  1.9 0.7 reshape.76.meta_ref
  2.6 129.0 %shard_map.91 = bf16[64,4096]{1,0:T(8,128)(2,1)} custom-call(bf16[64,4096]{1,0:T(8,128)(2,1)} %tok_ref.1, f32[4,16,256]{2,1,0:T(8,128)} %reshape.76.meta_ref, bf16[1,4096,768]{2,1,0:T(8,128)(2,1)} %gate_hbm.1, bf16[1,4096,768]{2,1,0:T(8,128)(2,1)} %up_hbm.1, bf16[1,768,4096]{2,1,0:T(8,128)(2,1)} %down_hbm.1, f32[1,768]{1,0:T(1,128)} %gate_scale_ref.1, ...), custom_call_target="tpu_custom_call" | custom-call | tf_op jit(solution)/shard_map/pallas_call | solution.py:345
  131.6 1.9 %copy.13 = bf16[64,4096]{1,0:T(8,128)(2,1)} copy(bf16[64,4096]{1,0:T(8,128)(2,1)} %shard_map.91) | data formatting | bytes 1048576
  (6 shorter events, 0.1 us)

commit v2 on v1

--- a/solution.py
+++ b/solution.py
@@ -20,6 +20,7 @@
 def kernel(
     groups,
     ring,
+    early,
     tok_ref,
     meta_ref,
     gate_hbm,
@@ -54,20 +55,31 @@
     out_p,
     in_p,
     own_p,
+    early_out_p,
+    early_in_p,
+    relay_z,
     back_out_p,
     back_in_p,
     back_own_p,
+    late_out_p,
+    late_in_p,
+    late_own_p,
     back_out_z,
     back_in_z,
-    back_own_z,
 ):
     chunks, _, cols = tokens.shape
     count = tok_ref.shape[0]
     members = metas.shape[1] // 2
-    slots = packed.shape[1] // members
+    first = members * early
+    slots = packed.shape[1] // members - early
+    away = 1 if early else 0
+    held = groups * count
     node, wide = lax.axis_index("node"), lax.axis_index("wide")
     my_group, my_ring = lax.div(wide, ring), lax.rem(wide, ring)
     me = node * ring + my_ring
+
+    is_end = jnp.logical_or(my_group == 0, my_group == groups - 1)
+    relays = groups == 4
 
     def group_at(i):
         return lax.rem(my_group + i, groups)
@@ -107,12 +119,14 @@
         w.start()
     pl.semaphore_wait(barrier, groups + members - 2)
 
+    half = tile_of(cols, 256)
+
     @pl.loop(1, groups)
     def _(i):
         g = group_at(i)
         pltpu.make_async_remote_copy(
             src_ref=meta_ref.at[g],
-            dst_ref=metas.at[my_group],
+            dst_ref=metas.at[groups - i],
             send_sem=meta_sems.at[0],
             recv_sem=meta_sems.at[1],
             device_id=group_id(g),
@@ -122,57 +136,114 @@
     @pl.loop(0, chunks)
     def _(c):
         mine = tok_ref.at[:, part(c, cols)]
-        place = tokens.at[c, part(my_group, count)]
 
         @pl.loop(1, groups)
         def _(i):
-            pltpu.make_async_remote_copy(
-                src_ref=mine,
-                dst_ref=place,
-                send_sem=out_z.at[c],
-                recv_sem=in_z.at[c],
-                device_id=group_id(group_at(i)),
-                device_id_type=MESH,
-            ).start()
-
-        pltpu.make_async_copy(mine, place, own_z.at[c]).start()
+            g = group_at(i)
+            direct = jnp.logical_not(jnp.logical_and(is_end, my_group + g == groups - 1))
+
+            @pl.when(jnp.logical_or(direct, not relays))
+            def _():
+                pltpu.make_async_remote_copy(
+                    src_ref=mine,
+                    dst_ref=tokens.at[c, part(groups - i, count)],
+                    send_sem=out_z.at[c],
+                    recv_sem=in_z.at[c],
+                    device_id=group_id(g),
+                    device_id_type=MESH,
+                ).start()
+
+        pltpu.make_async_copy(mine, tokens.at[c, pl.ds(0, count)], own_z.at[c]).start()
+
+    def fill(place, weight, at, base, size):
+        slot = base + lax.broadcasted_iota(jnp.int32, (size, held), 0).astype(jnp.float32)
+        for d in range(members):
+            same = place[d : d + 1, :] == slot
+            dispatch[pl.ds(at + d * size, size), :] = jnp.where(same, 1.0, 0.0).astype(jnp.bfloat16)
+            weighted[pl.ds(at + d * size, size), :] = jnp.where(same, weight[d : d + 1, :], 0.0)
+
+    metas[0] = meta_ref[my_group]
+    if early:
+        fill(metas[0, :members, :], metas[0, members:, :], 0, 0.0, early)
+
+        @pl.loop(0, chunks)
+        def _(c):
+            @pl.loop(0, cols // half)
+            def _(j):
+                packed[c, pl.ds(0, first), part(j, half)] = jnp.dot(
+                    dispatch[pl.ds(0, first), pl.ds(0, count)],
+                    tok_ref[:, part(c * (cols // half) + j, half)],
+                    preferred_element_type=jnp.float32,
+                ).astype(jnp.bfloat16)
+
+            @pl.loop(1, members)
+            def _(i):
+                d = member_at(i)
+                pltpu.make_async_remote_copy(
+                    src_ref=packed.at[c, part(d, early)],
+                    dst_ref=rows.at[c, part(me, early)],
+                    send_sem=early_out_p.at[c],
+                    recv_sem=early_in_p.at[c],
+                    device_id=member_id(d),
+                    device_id_type=MESH,
+                ).start()
 
     gate[...] = jnp.zeros_like(gate)
     up[...] = jnp.zeros_like(up)
 
-    own_meta = pltpu.make_async_copy(meta_ref.at[my_group], metas.at[my_group], meta_sems.at[2])
-    own_meta.start()
-    own_meta.wait()
-    arrived(metas.at[pl.ds(0, groups - 1)], meta_sems.at[1])
-    place = jnp.max(metas[:, :members, :], axis=0)
-    weight = jnp.sum(metas[:, members:, :], axis=0)
-    slot = lax.broadcasted_iota(jnp.int32, (slots, groups * count), 0).astype(jnp.float32)
-    for d in range(members):
-        same = place[d : d + 1, :] == slot
-        dispatch[pl.ds(d * slots, slots), :] = jnp.where(same, 1.0, 0.0).astype(jnp.bfloat16)
-        weighted[pl.ds(d * slots, slots), :] = jnp.where(same, weight[d : d + 1, :], 0.0)
+    arrived(metas.at[pl.ds(1, groups - 1)], meta_sems.at[1])
+    fill(
+        jnp.max(metas[:, :members, :], axis=0),
+        jnp.sum(metas[:, members:, :], axis=0),
+        first,
+        float(early),
+        slots,
+    )
     combine[...] = weighted[...].T.astype(jnp.bfloat16)
 
-    half = tile_of(cols, 256)
+    def rest(d):
+        return pl.ds(pl.multiple_of(first + d * slots, early or slots), slots)
+
+    def all_but_one(ref):
+        return ref.at[pl.ds(first, (members - 1) * slots)]
+
+    def early_but_one(ref):
+        return ref.at[pl.ds(0, (members - 1) * early)]
 
     def pack(c):
         pltpu.make_async_copy(
-            tok_ref.at[:, part(c, cols)], tokens.at[c, part(my_group, count)], own_z.at[c]
+            tok_ref.at[:, part(c, cols)], tokens.at[c, pl.ds(0, count)], own_z.at[c]
         ).wait()
-        arrived(tokens.at[c, pl.ds(0, (groups - 1) * count)], in_z.at[c])
+        arrived(tokens.at[c, pl.ds(count, (groups - 1) * count)], in_z.at[c])
+
+        if relays:
+            @pl.when(jnp.logical_not(is_end))
+            def _():
+                target = (groups - 1) * (my_group - 1)
+                distance = lax.rem(2 * groups - 1 - 2 * target, groups)
+                pltpu.make_async_remote_copy(
+                    src_ref=tokens.at[c, pl.ds(2 * count, count)],
+                    dst_ref=tokens.at[c, part(distance, count)],
+                    send_sem=relay_z.at[c],
+                    recv_sem=in_z.at[c],
+                    device_id=group_id(target),
+                    device_id_type=MESH,
+                ).start()
 
         @pl.loop(0, cols // half)
         def _(j):
-            packed[c, :, part(j, half)] = jnp.dot(
-                dispatch[...], tokens[c, :, part(j, half)], preferred_element_type=jnp.float32
+            packed[c, pl.ds(first, members * slots), part(j, half)] = jnp.dot(
+                dispatch[pl.ds(first, members * slots), :],
+                tokens[c, :, part(j, half)],
+                preferred_element_type=jnp.float32,
             ).astype(jnp.bfloat16)
 
         @pl.loop(1, members)
         def _(i):
             d = member_at(i)
             pltpu.make_async_remote_copy(
-                src_ref=packed.at[c, part(d, slots)],
-                dst_ref=rows.at[c, part(me, slots)],
+                src_ref=packed.at[c, rest(d)],
+                dst_ref=rows.at[c, rest(me)],
                 send_sem=out_p.at[c],
                 recv_sem=in_p.at[c],
                 device_id=member_id(d),
@@ -180,16 +251,19 @@
             ).start()
 
         pltpu.make_async_copy(
-            packed.at[c, part(me, slots)], rows.at[c, part(me, slots)], own_p.at[c]
+            packed.at[c, rest(me)], rows.at[c, rest(me)], own_p.at[c]
         ).start()
 
     wide_tile = tile_of(gate.shape[1], 256)
 
     def project(c):
         pltpu.make_async_copy(
-            packed.at[c, part(me, slots)], rows.at[c, part(me, slots)], own_p.at[c]
+            packed.at[c, rest(me)], rows.at[c, rest(me)], own_p.at[c]
         ).wait()
-        arrived(rows.at[c, pl.ds(0, (members - 1) * slots)], in_p.at[c])
+        if early:
+            rows[c, part(me, early), :] = packed[c, part(me, early), :]
+            arrived(early_but_one(rows.at[c]), early_in_p.at[c])
+        arrived(all_but_one(rows.at[c]), in_p.at[c])
 
         @pl.loop(0, gate.shape[1] // wide_tile)
         def _(j):
@@ -239,8 +313,8 @@
         def _(i):
             d = member_at(i)
             pltpu.make_async_remote_copy(
-                src_ref=results.at[c, part(d, slots)],
-                dst_ref=returned.at[c, part(me, slots)],
+                src_ref=results.at[c, rest(d)],
+                dst_ref=returned.at[c, rest(me)],
                 send_sem=back_out_p.at[c],
                 recv_sem=back_in_p.at[c],
                 device_id=member_id(d),
@@ -248,61 +322,91 @@
             ).start()
 
         pltpu.make_async_copy(
-            results.at[c, part(me, slots)], returned.at[c, part(me, slots)], back_own_p.at[c]
+            results.at[c, rest(me)], returned.at[c, rest(me)], back_own_p.at[c]
         ).start()
 
+    if early:
+
+        @pl.loop(0, chunks)
+        def _(c):
+            @pl.loop(1, members)
+            def _(i):
+                d = member_at(i)
+                pltpu.make_async_remote_copy(
+                    src_ref=results.at[c, part(d, early)],
+                    dst_ref=returned.at[c, part(me, early)],
+                    send_sem=late_out_p.at[c],
+                    recv_sem=late_in_p.at[c],
+                    device_id=member_id(d),
+                    device_id_type=MESH,
+                ).start()
+
     @pl.loop(0, chunks)
     def _(c):
         pltpu.make_async_copy(
-            results.at[c, part(me, slots)], returned.at[c, part(me, slots)], back_own_p.at[c]
+            results.at[c, rest(me)], returned.at[c, rest(me)], back_own_p.at[c]
         ).wait()
-        arrived(returned.at[c, pl.ds(0, (members - 1) * slots)], back_in_p.at[c])
+        arrived(all_but_one(returned.at[c]), back_in_p.at[c])
 
         @pl.loop(0, cols // half)
         def _(j):
-            partial[c, :, part(j, half)] = jnp.dot(
-                combine[...], returned[c, :, part(j, half)], preferred_element_type=jnp.float32
+            partial[c, pl.ds(away * count, held - away * count), part(j, half)] = jnp.dot(
+                combine[pl.ds(away * count, held - away * count), pl.ds(first, members * slots)],
+                returned[c, pl.ds(first, members * slots), part(j, half)],
+                preferred_element_type=jnp.float32,
             ).astype(jnp.bfloat16)
 
         @pl.loop(1, groups)
         def _(i):
-            g = group_at(i)
             pltpu.make_async_remote_copy(
-                src_ref=partial.at[c, part(g, count)],
-                dst_ref=partials.at[c, part(my_group, count)],
+                src_ref=partial.at[c, part(i, count)],
+                dst_ref=partials.at[c, part(groups - i, count)],
                 send_sem=back_out_z.at[c],
                 recv_sem=back_in_z.at[c],
-                device_id=group_id(g),
+                device_id=group_id(group_at(i)),
                 device_id_type=MESH,
             ).start()
 
-        pltpu.make_async_copy(
-            partial.at[c, part(my_group, count)],
-            partials.at[c, part(my_group, count)],
-            back_own_z.at[c],
-        ).start()
-
     @pl.loop(0, chunks)
     def _(c):
-        pltpu.make_async_copy(
-            partial.at[c, part(my_group, count)],
-            partials.at[c, part(my_group, count)],
-            back_own_z.at[c],
-        ).wait()
-        arrived(partials.at[c, pl.ds(0, (groups - 1) * count)], back_in_z.at[c])
-        total = partials[c, pl.ds(0, count), :].astype(jnp.float32)
+        if early:
+            returned[c, part(me, early), :] = results[c, part(me, early), :]
+            arrived(early_but_one(returned.at[c]), late_in_p.at[c])
+            total = jnp.dot(
+                combine[pl.ds(0, count), pl.ds(0, first)],
+                returned[c, pl.ds(0, first), :],
+                preferred_element_type=jnp.float32,
+            )
+        else:
+            total = partial[c, pl.ds(0, count), :].astype(jnp.float32)
+        arrived(partials.at[c, pl.ds(count, (groups - 1) * count)], back_in_z.at[c])
         for g in range(1, groups):
             total += partials[c, pl.ds(g * count, count), :].astype(jnp.float32)
         out_ref[:, part(c, cols)] = total.astype(jnp.bfloat16)
 
-    arrived(metas.at[pl.ds(0, groups - 1)], meta_sems.at[0])
+    arrived(metas.at[pl.ds(1, groups - 1)], meta_sems.at[0])
 
     @pl.loop(0, chunks)
     def _(c):
-        arrived(tokens.at[c, pl.ds(0, (groups - 1) * count)], out_z.at[c])
-        arrived(packed.at[c, pl.ds(0, (members - 1) * slots)], out_p.at[c])
-        arrived(results.at[c, pl.ds(0, (members - 1) * slots)], back_out_p.at[c])
-        arrived(partial.at[c, pl.ds(0, (groups - 1) * count)], back_out_z.at[c])
+        if relays:
+
+            @pl.when(is_end)
+            def _():
+                arrived(tokens.at[c, pl.ds(count, (groups - 2) * count)], out_z.at[c])
+
+            @pl.when(jnp.logical_not(is_end))
+            def _():
+                arrived(tokens.at[c, pl.ds(count, (groups - 1) * count)], out_z.at[c])
+                arrived(tokens.at[c, pl.ds(count, count)], relay_z.at[c])
+
+        else:
+            arrived(tokens.at[c, pl.ds(count, (groups - 1) * count)], out_z.at[c])
+        if early:
+            arrived(early_but_one(packed.at[c]), early_out_p.at[c])
+            arrived(early_but_one(results.at[c]), late_out_p.at[c])
+        arrived(all_but_one(packed.at[c]), out_p.at[c])
+        arrived(all_but_one(results.at[c]), back_out_p.at[c])
+        arrived(partial.at[c, pl.ds(count, (groups - 1) * count)], back_out_z.at[c])
 
 
 def on_device(
@@ -317,7 +421,7 @@
     groups = math.gcd(4, wides)
     ring = wides // groups
     members = nodes * ring
-    slots = groups * capacity
+    early = capacity if capacity % 16 == 0 and groups > 1 else 0
     held = groups * count
     chunks = CHUNKS
     cols = width // chunks
@@ -330,20 +434,26 @@
     position = jnp.dot(
         picked.astype(jnp.bfloat16), earlier.astype(jnp.bfloat16), preferred_element_type=jnp.float32
     )
-    place = jnp.where(picked, position + (my_group * capacity).astype(jnp.float32), -1.0)
-    here = (jnp.arange(held) // count == my_group)[None, :]
-    place = jnp.where(here, jnp.tile(place, (1, groups)), -1.0)
-    weight = jnp.where(here, jnp.tile(weight, (1, groups)), 0.0)
-    meta = jnp.stack([place, weight]).reshape(2, nodes, groups, ring, held)
-    meta = meta.transpose(2, 0, 1, 3, 4).reshape(groups, 2 * members, held)
+    distance = (my_group - jnp.arange(groups)) % groups
+    here = jnp.arange(held)[None, :] // count == distance[:, None]
+    start = (distance * capacity).astype(jnp.float32)
+
+    def tables(values):
+        values = values.reshape(nodes, groups, ring, count).transpose(1, 0, 2, 3)
+        return jnp.tile(values.reshape(groups, members, count), (1, 1, groups))
+
+    place = jnp.where(picked, position, -float(experts * count))
+    place = jnp.where(here[:, None, :], tables(place) + start[:, None, None], -1.0)
+    weight = jnp.where(here[:, None, :], tables(weight), 0.0)
+    meta = jnp.concatenate([place, weight], axis=1)
 
     vmem = pl.BlockSpec(memory_space=pltpu.VMEM)
     anywhere = pl.BlockSpec(memory_space=pl.ANY)
-    rows = members * slots
+    rows = members * groups * capacity
     bf16, f32 = jnp.bfloat16, jnp.float32
     per_chunk = pltpu.SemaphoreType.DMA((chunks,))
     return pl.pallas_call(
-        functools.partial(kernel, groups, ring),
+        functools.partial(kernel, groups, ring, early),
         out_shape=jax.ShapeDtypeStruct((count, width), bf16),
         in_specs=[vmem, vmem, anywhere, anywhere, anywhere, vmem, vmem, vmem],
         out_specs=vmem,
@@ -365,10 +475,10 @@
             pltpu.VMEM((rows, held), bf16),
             pltpu.VMEM((rows, held), f32),
             pltpu.VMEM((held, rows), bf16),
-            pltpu.SemaphoreType.DMA((3,)),
+            pltpu.SemaphoreType.DMA((2,)),
             pltpu.SemaphoreType.DMA((3,)),
         ]
-        + [per_chunk] * 12,
+        + [per_chunk] * 17,
         compiler_params=pltpu.CompilerParams(
             collective_id=0, has_side_effects=True, vmem_limit_bytes=60 * 2**20
         ),

time: 134 us -> 119 us (0.89)
  Pallas kernels: 129 us -> 114 us
    pallas_call x1, Pallas kernels: 129 us -> 114 us  [on_device(): pl.pallas_call(functools.partial(kernel, groups, ring, early), out_shape=...]
where the time goes in v2:
time: 119 us; the launch traced here: 118 us
  Pallas kernels  114 us (96%)
  other arithmetic  2.24 us (2%)
  local copies, waits for them, and re-layouts  2.12 us (2%)
    pallas_call x1, Pallas kernels, on_device(): pl.pallas_call(functools.partial(kernel, groups, ring, early), out_shape=...  114 us

profile of v2, /device:TPU:0, one launch (start us, length us, event | category | flops | bytes accessed | tf_op | source)
XLA Modules:
  0.0 118.4 jit_solution(6452430316547130497)
XLA Ops:
  0.0 0.1 broadcast_compare_fusion
  0.1 0.7 fusion
  0.8 0.1 convolution_select_fusion
  0.9 0.7 select_reduce_fusion
  1.7 0.1 tile.25
  1.8 0.1 tile.22
  1.9 0.1 add_select_fusion
  2.0 0.6 pad_maximum_fusion.meta_ref
  2.6 113.9 %shard_map.91 = bf16[64,4096]{1,0:T(8,128)(2,1)} custom-call(bf16[64,4096]{1,0:T(8,128)(2,1)} %tok_ref.1, f32[4,16,256]{2,1,0:T(8,128)} %pad_maximum_fusion.meta_ref, bf16[1,4096,768]{2,1,0:T(8,128)(2,1)} %gate_hbm.1, bf16[1,4096,768]{2,1,0:T(8,128)(2,1)} %up_hbm.1, bf16[1,768,4096]{2,1,0:T(8,128)(2,1)} %down_hbm.1, f32[1,768]{1,0:T(1,128)} %gate_scale_ref.1, ...), custom_call_target="tpu_custom_call" | custom-call | tf_op jit(solution)/shard_map/pallas_call | solution.py:455
  116.5 1.9 %copy.16 = bf16[64,4096]{1,0:T(8,128)(2,1)} copy(bf16[64,4096]{1,0:T(8,128)(2,1)} %shard_map.91) | data formatting | bytes 1048576
  (6 shorter events, 0.1 us)

commit v3 on v2

--- a/solution.py
+++ b/solution.py
@@ -44,6 +44,7 @@
     returned,
     partial,
     partials,
+    relayed,
     dispatch,
     weighted,
     combine,
@@ -66,6 +67,7 @@
     late_own_p,
     back_out_z,
     back_in_z,
+    back_relay_z,
 ):
     chunks, _, cols = tokens.shape
     count = tok_ref.shape[0]
@@ -341,6 +343,24 @@
                     device_id_type=MESH,
                 ).start()
 
+    def send_back(c, i):
+        pltpu.make_async_remote_copy(
+            src_ref=partial.at[c, part(i, count)],
+            dst_ref=partials.at[c, part(groups - i, count)],
+            send_sem=back_out_z.at[c],
+            recv_sem=back_in_z.at[c],
+            device_id=group_id(group_at(i)),
+            device_id_type=MESH,
+        ).start()
+
+    def add_and_send(c):
+        arrived(relayed.at[c], back_relay_z.at[c])
+        mine = partial[c, pl.ds(2 * count, count), :].astype(jnp.float32)
+        partial[c, pl.ds(2 * count, count), :] = (
+            mine + relayed[c].astype(jnp.float32)
+        ).astype(jnp.bfloat16)
+        send_back(c, 2)
+
     @pl.loop(0, chunks)
     def _(c):
         pltpu.make_async_copy(
@@ -358,14 +378,38 @@
 
         @pl.loop(1, groups)
         def _(i):
-            pltpu.make_async_remote_copy(
-                src_ref=partial.at[c, part(i, count)],
-                dst_ref=partials.at[c, part(groups - i, count)],
-                send_sem=back_out_z.at[c],
-                recv_sem=back_in_z.at[c],
-                device_id=group_id(group_at(i)),
-                device_id_type=MESH,
-            ).start()
+            g = group_at(i)
+            far = jnp.logical_and(is_end, my_group + g == groups - 1)
+            later = jnp.logical_and(jnp.logical_not(is_end), i == 2)
+
+            @pl.when(jnp.logical_or(not relays, jnp.logical_not(jnp.logical_or(far, later))))
+            def _():
+                send_back(c, i)
+
+            if relays:
+
+                @pl.when(far)
+                def _():
+                    pltpu.make_async_remote_copy(
+                        src_ref=partial.at[c, part(i, count)],
+                        dst_ref=relayed.at[c],
+                        send_sem=back_out_z.at[c],
+                        recv_sem=back_relay_z.at[c],
+                        device_id=group_id(1 + lax.div(my_group, groups - 1) * (groups - 3)),
+                        device_id_type=MESH,
+                    ).start()
+
+        if relays:
+
+            @pl.when(jnp.logical_and(jnp.logical_not(is_end), c > 0))
+            def _():
+                add_and_send(c - 1)
+
+    if relays:
+
+        @pl.when(jnp.logical_not(is_end))
+        def _():
+            add_and_send(chunks - 1)
 
     @pl.loop(0, chunks)
     def _(c):
@@ -379,7 +423,20 @@
             )
         else:
             total = partial[c, pl.ds(0, count), :].astype(jnp.float32)
-        arrived(partials.at[c, pl.ds(count, (groups - 1) * count)], back_in_z.at[c])
+        if relays:
+
+            @pl.when(is_end)
+            def _():
+                unused = 3 - 2 * lax.div(my_group, groups - 1)
+                partials[c, part(unused, count), :] = jnp.zeros((count, cols), jnp.bfloat16)
+                arrived(partials.at[c, pl.ds(0, (groups - 2) * count)], back_in_z.at[c])
+
+            @pl.when(jnp.logical_not(is_end))
+            def _():
+                arrived(partials.at[c, pl.ds(count, (groups - 1) * count)], back_in_z.at[c])
+
+        else:
+            arrived(partials.at[c, pl.ds(count, (groups - 1) * count)], back_in_z.at[c])
         for g in range(1, groups):
             total += partials[c, pl.ds(g * count, count), :].astype(jnp.float32)
         out_ref[:, part(c, cols)] = total.astype(jnp.bfloat16)
@@ -472,13 +529,14 @@
             pltpu.VMEM((chunks, rows, cols), bf16),
             pltpu.VMEM((chunks, held, cols), bf16),
             pltpu.VMEM((chunks, held, cols), bf16),
+            pltpu.VMEM((chunks, count, cols), bf16),
             pltpu.VMEM((rows, held), bf16),
             pltpu.VMEM((rows, held), f32),
             pltpu.VMEM((held, rows), bf16),
             pltpu.SemaphoreType.DMA((2,)),
             pltpu.SemaphoreType.DMA((3,)),
         ]
-        + [per_chunk] * 17,
+        + [per_chunk] * 18,
         compiler_params=pltpu.CompilerParams(
             collective_id=0, has_side_effects=True, vmem_limit_bytes=60 * 2**20
         ),

time: 119 us -> 119 us (level)
  no operation moved by 1% of the time
where the time goes in v3:
time: 119 us; the launch traced here: 118 us
  Pallas kernels  114 us (96%)
  other arithmetic  2.24 us (2%)
  local copies, waits for them, and re-layouts  2.12 us (2%)
    pallas_call x1, Pallas kernels, on_device(): pl.pallas_call(functools.partial(kernel, groups, ring, early), out_shape=...  114 us

profile of v3, /device:TPU:0, one launch (start us, length us, event | category | flops | bytes accessed | tf_op | source)
XLA Modules:
  0.0 118.5 jit_solution(7802256103603639572)
XLA Ops:
  0.0 0.1 broadcast_compare_fusion
  0.1 0.7 fusion
  0.8 0.1 convolution_select_fusion
  0.9 0.7 select_reduce_fusion
  1.7 0.1 tile.25
  1.8 0.1 tile.22
  1.9 0.1 add_select_fusion
  2.0 0.6 pad_maximum_fusion.meta_ref
  2.6 113.9 %shard_map.91 = bf16[64,4096]{1,0:T(8,128)(2,1)} custom-call(bf16[64,4096]{1,0:T(8,128)(2,1)} %tok_ref.1, f32[4,16,256]{2,1,0:T(8,128)} %pad_maximum_fusion.meta_ref, bf16[1,4096,768]{2,1,0:T(8,128)(2,1)} %gate_hbm.1, bf16[1,4096,768]{2,1,0:T(8,128)(2,1)} %up_hbm.1, bf16[1,768,4096]{2,1,0:T(8,128)(2,1)} %down_hbm.1, f32[1,768]{1,0:T(1,128)} %gate_scale_ref.1, ...), custom_call_target="tpu_custom_call" | custom-call | tf_op jit(solution)/shard_map/pallas_call | solution.py:512
  116.6 1.9 %copy.16 = bf16[64,4096]{1,0:T(8,128)(2,1)} copy(bf16[64,4096]{1,0:T(8,128)(2,1)} %shard_map.91) | data formatting | bytes 1048576
  (6 shorter events, 0.1 us)
